TPU v7x, 32 devices: a whole 2x2x4 slice. The times are simulated.
32 devices in a mesh: pair: 8 (over y, x, core), ladder: 4 (over z).
Axes of the slice: x: 2, y: 2, z: 4, core: 2. Of those that a mesh axis runs over, the one named last changes fastest.
Arguments:
- factors: bfloat16 [1536, 512, 512], P('pair', 'ladder'), may hold values from -0.0625 to 0.0625
- lambdas: bfloat16 [4, 512, 512], P(None, 'pair'), may hold values from -6 to 6
Outputs:
- residual: bfloat16 [512, 4, 512], P('pair', None, 'ladder')
All inputs are finite; a program needn't handle non-finite values.
Results may differ from a plain program's by a relative error of at most 0.013.
Values may be sent and summed in bfloat16 or wider, within the bound.
No kernel may reach another device: no remote copies, remote signals or barrier semaphores. Data moves between devices by JAX's collectives and lax.ppermute only.
A program may use at most 256 MiB of HBM per device.

v0:
```python
import functools

import jax
import jax.numpy as jnp
from jax import lax
from jax.experimental import pallas as pl
from jax.experimental.pallas import tpu as pltpu
from jax.sharding import PartitionSpec as P

F32 = jnp.float32
BF16 = jnp.bfloat16


def chunk_sizes(per_hub):
    sizes = []
    left = per_hub
    for share in (14, 12, 10, 6, 4):
        size = min(left, max(1, share * per_hub // 48))
        if size:
            sizes.append(size)
            left -= size
    if left:
        sizes.append(left)
    return sizes


def radices(count):
    steps = []
    while count > 1:
        step = 2 if not steps and count % 2 == 0 else next(r for r in (4, 2, 3, 5, count) if count % r == 0)
        steps.append(step)
        count //= step
    return steps


def turned(size, stride, radix, shift):
    perm = []
    for source in range(size):
        digit = source // stride % radix
        perm.append((source, source + ((digit + shift) % radix - digit) * stride))
    return perm


def products_kernel(cycle_scale, count, has_start, split, offset_ref, *refs):
    if split:
        *refs, keep_ref, send_ref, block_ref, turned_ref, cycle_ref, total_ref = refs
    else:
        *refs, total_ref, block_ref, turned_ref, cycle_ref = refs
    parts, lam_ref, lam_sum_ref = refs[:count], refs[count], refs[count + 1]
    group, rows, virt = parts[0].shape
    pairs = lam_ref.shape[0]

    @pl.when(pl.program_id(0) == 0)
    def _():
        total_ref[...] = refs[count + 2][...] if has_start else jnp.zeros_like(total_ref)
        cycle_ref[...] = jnp.zeros_like(cycle_ref)

    for q in range(group):
        for at, part in enumerate(parts):
            block_ref[q, at * rows : (at + 1) * rows, :] = part[q]
        turned_ref[q] = block_ref[q].T
        wide = block_ref[q].astype(F32)
        weight = jnp.sum(wide * lam_sum_ref[...], keepdims=True)
        cycle_ref[...] += weight * wide

    for pair in range(pairs):
        total = total_ref[pair]
        for q in range(group):
            half = jnp.dot(lam_ref[pair], turned_ref[q], preferred_element_type=F32).astype(BF16)
            total += jnp.dot(block_ref[q], half, preferred_element_type=F32)
        total_ref[pair] = total

    @pl.when(pl.program_id(0) == pl.num_programs(0) - 1)
    def _():
        cycle = cycle_ref[...].T.astype(BF16)
        for pair in range(pairs):
            for at in range(count):
                own = pl.ds(pl.multiple_of(offset_ref[1 + at], rows), rows)
                term = jnp.dot(lam_ref[pair, own, :], cycle, preferred_element_type=F32)
                total_ref[pair, at * rows : (at + 1) * rows, :] += cycle_scale * term
        if split:
            _, _, high, cols, _ = keep_ref.shape
            digit = offset_ref[1 + count]
            for pair in range(pairs):
                for at in range(count):
                    for place in range(high):
                        start = at * rows + 2 * place * cols
                        own = pl.ds(pl.multiple_of(start + digit * cols, cols), cols)
                        other = pl.ds(pl.multiple_of(start + (1 - digit) * cols, cols), cols)
                        keep_ref[pair, at, place] = total_ref[pair, own, :]
                        send_ref[pair, at, place] = total_ref[pair, other, :].astype(BF16)


def products(size, begin, offset, factors, near, far, lam_turned, lam_sum, total, halves=None):
    rows, virt = factors.shape[1:]
    pairs = lam_turned.shape[0]
    group = 1 if any(count % 2 for count in (size, begin, near.shape[0])) else 2
    first = begin // group
    whole = pl.BlockSpec((pairs, virt, virt), lambda p, o: (0, 0, 0))
    shape = (group, rows, virt)
    operands = [factors, near, *far, lam_turned, lam_sum]
    in_specs = [
        pl.BlockSpec(shape, lambda p, o: (o[0] // group + first + p, 0, 0)),
        pl.BlockSpec(shape, lambda p, o: (first + p, 0, 0)),
        *[pl.BlockSpec(shape, lambda p, o: (p, 0, 0)) for _ in far],
        whole,
        pl.BlockSpec((virt, virt), lambda p, o: (0, 0)),
    ]
    if total is not None:
        operands.append(total)
        in_specs.append(whole)
    scratch_shapes = [
        pltpu.VMEM((group, virt, virt), BF16),
        pltpu.VMEM((group, virt, virt), BF16),
        pltpu.VMEM((virt, virt), F32),
    ]
    if halves is None:
        out_specs, out_shape = whole, jax.ShapeDtypeStruct((pairs, virt, virt), F32)
    else:
        out_specs = [pl.BlockSpec(halves, lambda p, o: (0, 0, 0, 0, 0))] * 2
        out_shape = [jax.ShapeDtypeStruct(halves, F32), jax.ShapeDtypeStruct(halves, BF16)]
        scratch_shapes.append(pltpu.VMEM((pairs, virt, virt), F32))
    return pl.pallas_call(
        functools.partial(
            products_kernel, float(pairs * virt) ** (-0.5), 2 + len(far), total is not None, halves is not None
        ),
        grid_spec=pltpu.PrefetchScalarGridSpec(
            num_scalar_prefetch=1,
            grid=(size // group,),
            in_specs=in_specs,
            out_specs=out_specs,
            scratch_shapes=scratch_shapes,
        ),
        out_shape=out_shape,
        input_output_aliases={len(operands): 0} if total is not None and halves is None else {},
        compiler_params=pltpu.CompilerParams(vmem_limit_bytes=48 << 20),
        cost_estimate=pl.CostEstimate(flops=1, bytes_accessed=1, transcendentals=0),
    )(offset, *operands)


def per_device(pair_size, ladder_size, factors, lambdas):
    own_aux, rows, virt = factors.shape
    pairs = lambdas.shape[0]
    pair_index = lax.axis_index("pair")
    ladder_index = lax.axis_index("ladder")
    cols = virt // pair_size
    per_hub = own_aux // ladder_size
    sizes = chunk_sizes(per_hub)
    begins = [sum(sizes[:place]) for place in range(len(sizes))]

    def swap(array, flip):
        return lax.ppermute(array, "ladder", [(source, source ^ flip) for source in range(ladder_size)])

    def cut(index, flip, begin, size):
        return lax.dynamic_slice_in_dim(factors, (index ^ flip) * per_hub + begin, size, 0)

    flips = range(2, ladder_size)

    def exchange(place, index):
        return [swap(cut(index, flip, begins[place], sizes[place]), flip) for flip in flips]

    first = [cut(ladder_index, flip, begins[0], sizes[0]) for flip in flips]
    index, first = lax.optimization_barrier((ladder_index, first))
    far = [[swap(part, flip) for part, flip in zip(first, flips)]]
    second = [cut(index, flip, begins[1], sizes[1]) for flip in flips]
    index, second = lax.optimization_barrier((index, second))
    far.append([swap(part, flip) for part, flip in zip(second, flips)])

    near = swap(cut(index, 1, 0, per_hub), 1)
    lam_all = lax.all_gather(lambdas, "pair", axis=1, tiled=True)
    lam_turned = jnp.swapaxes(lam_all, 1, 2)
    places = [ladder_index * per_hub] + [(ladder_index ^ flip) * rows for flip in range(ladder_size)]
    offset = jnp.stack(places + [pair_index % 2]).astype(jnp.int32)
    lam_sum = jnp.sum(lam_all.astype(F32), axis=0)
    lam_sum = jnp.concatenate([lax.dynamic_slice_in_dim(lam_sum, start, rows, 0) for start in places[1:]])

    def digit_sum(total, stride, low, radix):
        digit = pair_index // stride % radix
        view = total.reshape(pairs, ladder_size, low // radix, radix, cols, virt)
        total = lax.dynamic_index_in_dim(view, digit, 3, keepdims=False)
        for shift in range(1, radix):
            part = lax.dynamic_index_in_dim(view, (digit + shift) % radix, 3, keepdims=False)
            part = lax.ppermute(part.astype(BF16), "pair", turned(pair_size, stride, radix, shift))
            total = total + part.astype(F32)
        return total

    low = pair_size // ladder_size
    steps = radices(low)
    halves = None
    if steps[:1] == [2] and cols % 16 == 0:
        halves = (pairs, ladder_size, low // 2, cols, virt)

    total = None
    for place, size in enumerate(sizes):
        if place + 2 < len(sizes):
            if place:
                index, total = lax.optimization_barrier((index, total))
            index, far[place] = lax.optimization_barrier((index, far[place]))
            far.append(exchange(place + 2, index))
        total = products(
            size, begins[place], offset, factors, near, far[place], lam_turned, lam_sum, total,
            halves if place + 1 == len(sizes) else None,
        )

    stride = 1
    if halves:
        keep, send = total
        total = keep + lax.ppermute(send, "pair", turned(pair_size, 1, 2, 1)).astype(F32)
        stride, low, steps = 2, low // 2, steps[1:]
    for radix in steps:
        total = digit_sum(total, stride, low, radix)
        stride, low = stride * radix, low // radix
    digit = pair_index // stride
    view = total.reshape(pairs, ladder_size, cols, virt)
    total = None
    for flip in range(ladder_size):
        part = lax.dynamic_index_in_dim(view, ladder_index ^ digit ^ flip, 1, keepdims=False)
        if flip:
            perm = [(source, source ^ (flip * stride)) for source in range(pair_size)]
            part = lax.ppermute(part.astype(BF16), "pair", perm).astype(F32)
        total = part if total is None else total + part

    result = None
    for flip in range(ladder_size):
        part = lax.slice_in_dim(total, flip * rows, (flip + 1) * rows, axis=2)
        if flip:
            part = swap(part.astype(BF16), flip).astype(F32)
        result = part if result is None else result + part
    return jnp.swapaxes(result.astype(BF16), 0, 1)


def solution(mesh):
    in_specs = (P("pair", "ladder", None), P(None, "pair", None))
    out_specs = P("pair", None, "ladder")
    body = functools.partial(per_device, mesh.shape["pair"], mesh.shape["ladder"])
    return jax.shard_map(body, mesh=mesh, in_specs=in_specs, out_specs=out_specs, check_vma=False)
```

profile of v0, /device:TPU:0, one launch (start us, length us, event | category | flops | bytes accessed | tf_op | source)
XLA Modules:
  0.0 624.4 jit_solution(10985343488174134804)
XLA Ops:
  6.5 4.3 constant_dynamic-slice_fusion.15
  10.8 3.9 constant_dynamic-slice_fusion.13
  14.7 6.2 constant_dynamic-slice_fusion.12
  20.9 3.0 collective-permute-start
  24.8 2.7 collective-permute-start.1
  27.5 1.9 collective-permute-start.3
  29.4 1.9 collective-permute-start.4
  31.3 168.2 %collective-permute-done.1.refs_2_ = bf16[14,128,512]{2,1,0:T(8,128)(2,1)S(1)} collective-permute-done((bf16[14,128,512]{2,1,0:T(8,128)(2,1)}, bf16[14,128,512]{2,1,0:T(8,128)(2,1)S(1)}, u32[]{:S(2)}, u32[]{:S(2)}) %collective-permute-start.1) | collective-permute-done | bytes 1835040 | tf_op jit(solution)/shard_map/ppermute | solution.py:152
  199.5 42.2 %collective-permute-done.2.refs_3_ = bf16[14,128,512]{2,1,0:T(8,128)(2,1)S(1)} collective-permute-done((bf16[14,128,512]{2,1,0:T(8,128)(2,1)}, bf16[14,128,512]{2,1,0:T(8,128)(2,1)S(1)}, u32[]{:S(2)}, u32[]{:S(2)}) %collective-permute-start.2) | collective-permute-done | bytes 1835040 | tf_op jit(solution)/shard_map/ppermute | solution.py:152
  243.0 3.6 constant_dynamic-slice_fusion.6
  248.0 4.3 copy.22
  252.2 2.1 convert_reduce_fusion
  254.5 17.6 %collective-permute-done.refs_1_ = bf16[48,128,512]{2,1,0:T(8,128)(2,1)} collective-permute-done((bf16[48,128,512]{2,1,0:T(8,128)(2,1)}, bf16[48,128,512]{2,1,0:T(8,128)(2,1)}, u32[]{:S(2)}, u32[]{:S(2)}) %collective-permute-start) | collective-permute-done | bytes 6291488 | tf_op jit(solution)/shard_map/ppermute | solution.py:152
  272.1 45.0 %shard_map.28.refs_6_ = f32[4,512,512]{2,1,0:T(8,128)} custom-call(s32[6]{0:T(128)S(1)} %stack.27.offset_ref, bf16[192,128,512]{2,1,0:T(8,128)(2,1)} %refs_0_.11, bf16[48,128,512]{2,1,0:T(8,128)(2,1)} %collective-permute-done.refs_1_, bf16[14,128,512]{2,1,0:T(8,128)(2,1)S(1)} %collective-permute-done.1.refs_2_, bf16[14,128,512]{2,1,0:T(8,128)(2,1)S(1)} %copy-done.2, ...), custom_call_target="tpu_custom_call" | custom-call | flops 1 | bytes 1 | tf_op jit(solution)/shard_map/pallas_call | solution.py:123
  317.1 2.6 constant_dynamic-slice_fusion.4
  319.8 62.5 %collective-permute-start.7 = (bf16[6,128,512]{2,1,0:T(8,128)(2,1)}, bf16[6,128,512]{2,1,0:T(8,128)(2,1)}, u32[]{:S(2)}, u32[]{:S(2)}) collective-permute-start(bf16[6,128,512]{2,1,0:T(8,128)(2,1)} %get-tuple-element.64), channel_id=1, source_target_pairs={{0,2},{1,3},{2,0},{3,1},{4,6},{5,7},{6,4},{7,5},{8,10},{9,11},{10,... | collective-permute-start | bytes 2359304 | tf_op jit(solution)/shard_map/ppermute | solution.py:152
  383.6 41.4 %shard_map.29.refs_6_ = f32[4,512,512]{2,1,0:T(8,128)} custom-call(s32[6]{0:T(128)S(1)} %stack.27.offset_ref, bf16[192,128,512]{2,1,0:T(8,128)(2,1)} %refs_0_.11, bf16[48,128,512]{2,1,0:T(8,128)(2,1)} %collective-permute-done.refs_1_, bf16[12,128,512]{2,1,0:T(8,128)(2,1)} %collective-permute-done.3.refs_2_, ...), custom_call_target="tpu_custom_call", output_to_operand_aliasing={{}: (7, {})} | custom-call | flops 1 | bytes 1 | tf_op jit(solution)/shard_map/pallas_call | solution.py:123
  425.0 14.9 %collective-permute-done.5.refs_2_ = bf16[10,128,512]{2,1,0:T(8,128)(2,1)} collective-permute-done((bf16[10,128,512]{2,1,0:T(8,128)(2,1)}, bf16[10,128,512]{2,1,0:T(8,128)(2,1)}, u32[]{:S(2)}, u32[]{:S(2)}) %collective-permute-start.5) | collective-permute-done | bytes 1310752 | tf_op jit(solution)/shard_map/ppermute | solution.py:152
  439.9 2.3 constant_dynamic-slice_fusion
  442.2 29.7 %collective-permute-start.11 = (bf16[4,128,512]{2,1,0:T(8,128)(2,1)}, bf16[4,128,512]{2,1,0:T(8,128)(2,1)}, u32[]{:S(2)}, u32[]{:S(2)}) collective-permute-start(bf16[4,128,512]{2,1,0:T(8,128)(2,1)} %get-tuple-element.60), channel_id=1, source_target_pairs={{0,2},{1,3},{2,0},{3,1},{4,6},{5,7},{6,4},{7,5},{8,10},{9,11},{10,... | collective-permute-start | bytes 1572872 | tf_op jit(solution)/shard_map/ppermute | solution.py:152
  473.2 35.4 %shard_map.30.refs_6_ = f32[4,512,512]{2,1,0:T(8,128)} custom-call(s32[6]{0:T(128)S(1)} %stack.27.offset_ref, bf16[192,128,512]{2,1,0:T(8,128)(2,1)} %refs_0_.11, bf16[48,128,512]{2,1,0:T(8,128)(2,1)} %collective-permute-done.refs_1_, bf16[10,128,512]{2,1,0:T(8,128)(2,1)} %collective-permute-done.5.refs_2_, ...), custom_call_target="tpu_custom_call", output_to_operand_aliasing={{}: (7, {})} | custom-call | flops 1 | bytes 1 | tf_op jit(solution)/shard_map/pallas_call | solution.py:123
  509.7 17.2 %collective-permute-start.9 = (bf16[2,128,512]{2,1,0:T(8,128)(2,1)S(1)}, bf16[2,128,512]{2,1,0:T(8,128)(2,1)S(1)}, u32[]{:S(2)}, u32[]{:S(2)}) collective-permute-start(bf16[2,128,512]{2,1,0:T(8,128)(2,1)S(1)} %get-tuple-element.62), channel_id=1, source_target_pairs={{0,2},{1,3},{2,0},{3,1},{4,6},{5,7},{6,4},{7,5},{8,10},{9,11},{10,... | collective-permute-start | bytes 786440 | tf_op jit(solution)/shard_map/ppermute | solution.py:152
  528.2 23.8 %shard_map.31.refs_6_ = f32[4,512,512]{2,1,0:T(8,128)} custom-call(s32[6]{0:T(128)S(1)} %stack.27.offset_ref, bf16[192,128,512]{2,1,0:T(8,128)(2,1)} %refs_0_.11, bf16[48,128,512]{2,1,0:T(8,128)(2,1)} %collective-permute-done.refs_1_, bf16[6,128,512]{2,1,0:T(8,128)(2,1)} %collective-permute-done.7.refs_2_, ...), custom_call_target="tpu_custom_call", output_to_operand_aliasing={{}: (7, {})} | custom-call | flops 1 | bytes 1 | tf_op jit(solution)/shard_map/pallas_call | solution.py:123
  552.0 18.5 %shard_map.32.refs_6_ = f32[4,512,512]{2,1,0:T(8,128)} custom-call(s32[6]{0:T(128)S(1)} %stack.27.offset_ref, bf16[192,128,512]{2,1,0:T(8,128)(2,1)} %refs_0_.11, bf16[48,128,512]{2,1,0:T(8,128)(2,1)} %collective-permute-done.refs_1_, bf16[4,128,512]{2,1,0:T(8,128)(2,1)} %collective-permute-done.11.refs_2_, ...), custom_call_target="tpu_custom_call", output_to_operand_aliasing={{}: (7, {})} | custom-call | flops 1 | bytes 1 | tf_op jit(solution)/shard_map/pallas_call | solution.py:123
  570.6 11.0 %shard_map.33 = (f32[4,4,1,64,512]{4,3,2,1,0:T(8,128)S(1)}, bf16[4,4,1,64,512]{4,3,2,1,0:T(8,128)(2,1)}) custom-call(s32[6]{0:T(128)S(1)} %stack.27.offset_ref, bf16[192,128,512]{2,1,0:T(8,128)(2,1)} %refs_0_.11, bf16[48,128,512]{2,1,0:T(8,128)(2,1)} %collective-permute-done.refs_1_, bf16[2,128,512]{2,1,0:T(8,128)(2,1)S(1)} %collective-permute-done.9.refs_2_, ...), custom_call_target="tpu_custom_call" | custom-call | flops 1 | bytes 1 | tf_op jit(solution)/shard_map/pallas_call | solution.py:123
  581.6 2.9 collective-permute-done.13
  587.7 2.5 collective-permute-start.16
  591.3 6.6 %collective-permute-done.16 = bf16[4,64,512]{2,1,0:T(8,128)(2,1)S(1)} collective-permute-done((bf16[4,64,512]{2,1,0:T(8,128)(2,1)S(1)}, bf16[4,64,512]{2,1,0:T(8,128)(2,1)S(1)}, u32[]{:S(2)}, u32[]{:S(2)}) %collective-permute-start.16) | collective-permute-done | bytes 262176 | tf_op jit(solution)/shard_map/ppermute | solution.py:220
  597.9 4.8 collective-permute-done.15
  604.0 2.5 collective-permute-start.19
  606.5 5.4 collective-permute-start.18
  612.0 3.9 collective-permute-done.18
  (44 shorter events, 16.1 us)
Async XLA Ops:
  6.5 241.5 %all-gather.2.cloned.1.call-start = ((), (), s32[]{:S(2)}) async-start(), calls=%async_computation | async-start | bytes 2359296 | tf_op jit(solution)/shard_map/all_gather | solution.py:170
  14.7 9.2 %copy-start.3 = (bf16[4,64,512]{2,1,0:T(8,128)(2,1)S(1)}, bf16[4,64,512]{2,1,0:T(8,128)(2,1)}, u32[]{:S(2)}) copy-start(bf16[4,64,512]{2,1,0:T(8,128)(2,1)} %param.3) | copy-start | bytes 786436
  20.9 251.2 %collective-permute-start = (bf16[48,128,512]{2,1,0:T(8,128)(2,1)}, bf16[48,128,512]{2,1,0:T(8,128)(2,1)}, u32[]{:S(2)}, u32[]{:S(2)}) collective-permute-start(bf16[48,128,512]{2,1,0:T(8,128)(2,1)} %constant_dynamic-slice_fusion.12), channel_id=1, source_target_pairs={{0,1},{1,0},{2,3},{3,2},{4,5},{5,4},{6,7},{7,6},{8,9},{9,8},{10,11... | collective-permute-start | bytes 18874376 | tf_op jit(solution)/shard_map/ppermute | solution.py:152
  24.8 174.7 %collective-permute-start.1 = (bf16[14,128,512]{2,1,0:T(8,128)(2,1)}, bf16[14,128,512]{2,1,0:T(8,128)(2,1)S(1)}, u32[]{:S(2)}, u32[]{:S(2)}) collective-permute-start(bf16[14,128,512]{2,1,0:T(8,128)(2,1)} %get-tuple-element.33), channel_id=1, source_target_pairs={{0,2},{1,3},{2,0},{3,1},{4,6},{5,7},{6,4},{7,5},{8,10},{9,11},{10,... | collective-permute-start | bytes 5505032 | tf_op jit(solution)/shard_map/ppermute | solution.py:152
  27.5 214.3 %collective-permute-start.2 = (bf16[14,128,512]{2,1,0:T(8,128)(2,1)}, bf16[14,128,512]{2,1,0:T(8,128)(2,1)S(1)}, u32[]{:S(2)}, u32[]{:S(2)}) collective-permute-start(bf16[14,128,512]{2,1,0:T(8,128)(2,1)} %get-tuple-element.34), channel_id=1, source_target_pairs={{0,3},{1,2},{2,1},{3,0},{4,7},{5,6},{6,5},{7,4},{8,11},{9,10},{10,... | collective-permute-start | bytes 5505032 | tf_op jit(solution)/shard_map/ppermute | solution.py:152
  27.5 289.6 %collective-permute-start.3 = (bf16[12,128,512]{2,1,0:T(8,128)(2,1)}, bf16[12,128,512]{2,1,0:T(8,128)(2,1)}, u32[]{:S(2)}, u32[]{:S(2)}) collective-permute-start(bf16[12,128,512]{2,1,0:T(8,128)(2,1)} %get-tuple-element.39), channel_id=1, source_target_pairs={{0,2},{1,3},{2,0},{3,1},{4,6},{5,7},{6,4},{7,5},{8,10},{9,11},{10,... | collective-permute-start | bytes 4718600 | tf_op jit(solution)/shard_map/ppermute | solution.py:152
  29.4 287.7 %collective-permute-start.4 = (bf16[12,128,512]{2,1,0:T(8,128)(2,1)}, bf16[12,128,512]{2,1,0:T(8,128)(2,1)}, u32[]{:S(2)}, u32[]{:S(2)}) collective-permute-start(bf16[12,128,512]{2,1,0:T(8,128)(2,1)} %get-tuple-element.40), channel_id=1, source_target_pairs={{0,3},{1,2},{2,1},{3,0},{4,7},{5,6},{6,5},{7,4},{8,11},{9,10},{10,... | collective-permute-start | bytes 4718600 | tf_op jit(solution)/shard_map/ppermute | solution.py:152
  241.7 1.3 copy-start.1
  246.6 193.3 %collective-permute-start.5 = (bf16[10,128,512]{2,1,0:T(8,128)(2,1)}, bf16[10,128,512]{2,1,0:T(8,128)(2,1)}, u32[]{:S(2)}, u32[]{:S(2)}) collective-permute-start(bf16[10,128,512]{2,1,0:T(8,128)(2,1)} %get-tuple-element.66), channel_id=1, source_target_pairs={{0,2},{1,3},{2,0},{3,1},{4,6},{5,7},{6,4},{7,5},{8,10},{9,11},{10,... | collective-permute-start | bytes 3932168 | tf_op jit(solution)/shard_map/ppermute | solution.py:152
  246.6 193.3 %collective-permute-start.6 = (bf16[10,128,512]{2,1,0:T(8,128)(2,1)}, bf16[10,128,512]{2,1,0:T(8,128)(2,1)}, u32[]{:S(2)}, u32[]{:S(2)}) collective-permute-start(bf16[10,128,512]{2,1,0:T(8,128)(2,1)} %get-tuple-element.65), channel_id=1, source_target_pairs={{0,3},{1,2},{2,1},{3,0},{4,7},{5,6},{6,5},{7,4},{8,11},{9,10},{10,... | collective-permute-start | bytes 3932168 | tf_op jit(solution)/shard_map/ppermute | solution.py:152
  254.3 17.8 %copy-start.2 = (bf16[14,128,512]{2,1,0:T(8,128)(2,1)S(1)}, bf16[14,128,512]{2,1,0:T(8,128)(2,1)}, u32[]{:S(2)}) copy-start(bf16[14,128,512]{2,1,0:T(8,128)(2,1)} %copy-done.1) | copy-start | bytes 5505028
  319.8 188.8 %collective-permute-start.7 = (bf16[6,128,512]{2,1,0:T(8,128)(2,1)}, bf16[6,128,512]{2,1,0:T(8,128)(2,1)}, u32[]{:S(2)}, u32[]{:S(2)}) collective-permute-start(bf16[6,128,512]{2,1,0:T(8,128)(2,1)} %get-tuple-element.64), channel_id=1, source_target_pairs={{0,2},{1,3},{2,0},{3,1},{4,6},{5,7},{6,4},{7,5},{8,10},{9,11},{10,... | collective-permute-start | bytes 2359304 | tf_op jit(solution)/shard_map/ppermute | solution.py:152
  382.3 126.3 %collective-permute-start.8 = (bf16[6,128,512]{2,1,0:T(8,128)(2,1)}, bf16[6,128,512]{2,1,0:T(8,128)(2,1)}, u32[]{:S(2)}, u32[]{:S(2)}) collective-permute-start(bf16[6,128,512]{2,1,0:T(8,128)(2,1)} %get-tuple-element.63), channel_id=1, source_target_pairs={{0,3},{1,2},{2,1},{3,0},{4,7},{5,6},{6,5},{7,4},{8,11},{9,10},{10,... | collective-permute-start | bytes 2359304 | tf_op jit(solution)/shard_map/ppermute | solution.py:152
  425.0 48.2 %copy-start = (bf16[4,512,512]{1,2,0:T(8,128)(2,1)S(1)}, bf16[4,512,512]{1,2,0:T(8,128)(2,1)}, u32[]{:S(2)}) copy-start(bf16[4,512,512]{1,2,0:T(8,128)(2,1)} %copy.22) | copy-start | bytes 6291460
  442.2 109.8 %collective-permute-start.11 = (bf16[4,128,512]{2,1,0:T(8,128)(2,1)}, bf16[4,128,512]{2,1,0:T(8,128)(2,1)}, u32[]{:S(2)}, u32[]{:S(2)}) collective-permute-start(bf16[4,128,512]{2,1,0:T(8,128)(2,1)} %get-tuple-element.60), channel_id=1, source_target_pairs={{0,2},{1,3},{2,0},{3,1},{4,6},{5,7},{6,4},{7,5},{8,10},{9,11},{10,... | collective-permute-start | bytes 1572872 | tf_op jit(solution)/shard_map/ppermute | solution.py:152
  471.8 80.2 %collective-permute-start.12 = (bf16[4,128,512]{2,1,0:T(8,128)(2,1)}, bf16[4,128,512]{2,1,0:T(8,128)(2,1)}, u32[]{:S(2)}, u32[]{:S(2)}) collective-permute-start(bf16[4,128,512]{2,1,0:T(8,128)(2,1)} %get-tuple-element.59), channel_id=1, source_target_pairs={{0,3},{1,2},{2,1},{3,0},{4,7},{5,6},{6,5},{7,4},{8,11},{9,10},{10,... | collective-permute-start | bytes 1572872 | tf_op jit(solution)/shard_map/ppermute | solution.py:152
  509.7 60.9 %collective-permute-start.9 = (bf16[2,128,512]{2,1,0:T(8,128)(2,1)S(1)}, bf16[2,128,512]{2,1,0:T(8,128)(2,1)S(1)}, u32[]{:S(2)}, u32[]{:S(2)}) collective-permute-start(bf16[2,128,512]{2,1,0:T(8,128)(2,1)S(1)} %get-tuple-element.62), channel_id=1, source_target_pairs={{0,2},{1,3},{2,0},{3,1},{4,6},{5,7},{6,4},{7,5},{8,10},{9,11},{10,... | collective-permute-start | bytes 786440 | tf_op jit(solution)/shard_map/ppermute | solution.py:152
  526.8 43.7 %collective-permute-start.10 = (bf16[2,128,512]{2,1,0:T(8,128)(2,1)S(1)}, bf16[2,128,512]{2,1,0:T(8,128)(2,1)S(1)}, u32[]{:S(2)}, u32[]{:S(2)}) collective-permute-start(bf16[2,128,512]{2,1,0:T(8,128)(2,1)S(1)} %get-tuple-element.61), channel_id=1, source_target_pairs={{0,3},{1,2},{2,1},{3,0},{4,7},{5,6},{6,5},{7,4},{8,11},{9,10},{10,... | collective-permute-start | bytes 786440 | tf_op jit(solution)/shard_map/ppermute | solution.py:152
  581.6 2.9 collective-permute-start.13
  587.7 10.2 %collective-permute-start.16 = (bf16[4,64,512]{2,1,0:T(8,128)(2,1)S(1)}, bf16[4,64,512]{2,1,0:T(8,128)(2,1)S(1)}, u32[]{:S(2)}, u32[]{:S(2)}) collective-permute-start(bf16[4,64,512]{2,1,0:T(8,128)(2,1)S(1)} %get-tuple-element.72), channel_id=1, source_target_pairs={{0,24},{4,28},{8,16},{12,20},{16,8},{20,12},{24,0},{28,4},{1,25},{... | collective-permute-start | bytes 786440 | tf_op jit(solution)/shard_map/ppermute | solution.py:220
  590.2 12.4 %collective-permute-start.15 = (bf16[4,64,512]{2,1,0:T(8,128)(2,1)S(1)}, bf16[4,64,512]{2,1,0:T(8,128)(2,1)S(1)}, u32[]{:S(2)}, u32[]{:S(2)}) collective-permute-start(bf16[4,64,512]{2,1,0:T(8,128)(2,1)S(1)} %get-tuple-element.73), channel_id=1, source_target_pairs={{0,16},{4,20},{8,24},{12,28},{16,0},{20,4},{24,8},{28,12},{1,17},{... | collective-permute-start | bytes 786440 | tf_op jit(solution)/shard_map/ppermute | solution.py:220
  590.7 12.0 %collective-permute-start.14 = (bf16[4,64,512]{2,1,0:T(8,128)(2,1)S(1)}, bf16[4,64,512]{2,1,0:T(8,128)(2,1)S(1)}, u32[]{:S(2)}, u32[]{:S(2)}) collective-permute-start(bf16[4,64,512]{2,1,0:T(8,128)(2,1)S(1)} %get-tuple-element.71), channel_id=1, source_target_pairs={{0,8},{4,12},{8,0},{12,4},{16,24},{20,28},{24,16},{28,20},{1,9},{5... | collective-permute-start | bytes 786440 | tf_op jit(solution)/shard_map/ppermute | solution.py:220
  604.0 8.0 %collective-permute-start.19 = (bf16[4,64,128]{2,1,0:T(8,128)(2,1)S(1)}, bf16[4,64,128]{2,1,0:T(8,128)(2,1)S(1)}, u32[]{:S(2)}, u32[]{:S(2)}) collective-permute-start(bf16[4,64,128]{2,1,0:T(8,128)(2,1)S(1)} %get-tuple-element.79), channel_id=1, source_target_pairs={{0,3},{1,2},{2,1},{3,0},{4,7},{5,6},{6,5},{7,4},{8,11},{9,10},{10,... | collective-permute-start | bytes 196616 | tf_op jit(solution)/shard_map/ppermute | solution.py:152
  606.5 9.4 %collective-permute-start.18 = (bf16[4,64,128]{2,1,0:T(8,128)(2,1)S(1)}, bf16[4,64,128]{2,1,0:T(8,128)(2,1)S(1)}, u32[]{:S(2)}, u32[]{:S(2)}) collective-permute-start(bf16[4,64,128]{2,1,0:T(8,128)(2,1)S(1)} %get-tuple-element.80), channel_id=1, source_target_pairs={{0,2},{1,3},{2,0},{3,1},{4,6},{5,7},{6,4},{7,5},{8,10},{9,11},{10,... | collective-permute-start | bytes 196616 | tf_op jit(solution)/shard_map/ppermute | solution.py:152
  611.9 4.7 collective-permute-start.17
Sparse Core Ops, SparseCore 0:
  24.9 28.1 all-gather.1
where the time goes:
time: 632 us; the launch traced here: 624 us
  waiting for transfers between devices  262 us (41%)
  Pallas kernels  175 us (28%)
  starting transfers between devices  136 us (22%)
  local copies, waits for them, and re-layouts  32.7 us (5%)
  between operations  13.8 us (2%)
    ppermute x16, waiting for transfers between devices, swap(): lax.ppermute(array, 'ladder', [(source, source ^ flip) for source in rang...  247 us
    pallas_call x6, Pallas kernels, products(): pl.pallas_call(functools.partial(products_kernel, float(pairs * virt) **...  175 us
    ppermute x16, starting transfers between devices, swap(): lax.ppermute(array, 'ladder', [(source, source ^ flip) for source in rang...  132 us
    dynamic_slice x7, local copies, waits for them, and re-layouts, cut(): lax.dynamic_slice_in_dim(factors, (index ^ flip) * per_hub + begin, size, 0)  23.9 us
  transfers between devices with their start and end apart: 21, of which 10 were waited for; matrix products, arithmetic and copies ran while one was open for 3% of the time, Pallas kernels for 26%

commit v1 on v0

--- a/solution.py
+++ b/solution.py
@@ -14,7 +14,7 @@
 def chunk_sizes(per_hub):
     sizes = []
     left = per_hub
-    for share in (14, 12, 10, 6, 4):
+    for share in (4, 14, 12, 10, 6):
         size = min(left, max(1, share * per_hub // 48))
         if size:
             sizes.append(size)
@@ -160,18 +160,19 @@
         return [swap(cut(index, flip, begins[place], sizes[place]), flip) for flip in flips]
 
     first = [cut(ladder_index, flip, begins[0], sizes[0]) for flip in flips]
+    far = [[swap(part, flip) for part, flip in zip(first, flips)]]
+    lam_all = lax.all_gather(lambdas, "pair", axis=1, tiled=True)
     index, first = lax.optimization_barrier((ladder_index, first))
-    far = [[swap(part, flip) for part, flip in zip(first, flips)]]
-    second = [cut(index, flip, begins[1], sizes[1]) for flip in flips]
-    index, second = lax.optimization_barrier((index, second))
-    far.append([swap(part, flip) for part, flip in zip(second, flips)])
-
-    near = swap(cut(index, 1, 0, per_hub), 1)
-    lam_all = lax.all_gather(lambdas, "pair", axis=1, tiled=True)
+    second = [cut(index, 1, 0, per_hub)] + [cut(index, flip, begins[1], sizes[1]) for flip in flips]
+    lam_all, second = lax.optimization_barrier((lam_all, second))
     lam_turned = jnp.swapaxes(lam_all, 1, 2)
+    lam_sum = jnp.sum(lam_all.astype(F32), axis=0)
+    second, far[0] = lax.optimization_barrier((second, far[0]))
+    near, *others = [swap(part, flip) for flip, part in enumerate(second, 1)]
+    far.append(others)
+
     places = [ladder_index * per_hub] + [(ladder_index ^ flip) * rows for flip in range(ladder_size)]
     offset = jnp.stack(places + [pair_index % 2]).astype(jnp.int32)
-    lam_sum = jnp.sum(lam_all.astype(F32), axis=0)
     lam_sum = jnp.concatenate([lax.dynamic_slice_in_dim(lam_sum, start, rows, 0) for start in places[1:]])
 
     def digit_sum(total, stride, low, radix):

time: 632 us -> 629 us (level)
  starting transfers between devices: 136 us -> 106 us
  waiting for transfers between devices: 262 us -> 286 us
    ppermute x16, starting transfers between devices: 132 us -> 103 us  [swap(): lax.ppermute(array, 'ladder', [(source, source ^ flip) for source in rang...]
    all_gather x1, waiting for transfers between devices: 0.01 us -> 14.2 us  [per_device(): lam_all = lax.all_gather(lambdas, 'pair', axis=1, tiled=True)]
    ppermute x16, waiting for transfers between devices: 247 us -> 258 us  [swap(): lax.ppermute(array, 'ladder', [(source, source ^ flip) for source in rang...]
  transfers between devices with their start and end apart: 21 -> 21, of which waited for: 10 -> 10; matrix products, arithmetic and copies ran while one was open for 3% -> 5% of each run, Pallas kernels for 26% -> 27%
where the time goes in v1:
time: 629 us; the launch traced here: 620 us
  waiting for transfers between devices  286 us (45%)
  Pallas kernels  176 us (28%)
  starting transfers between devices  106 us (17%)
  local copies, waits for them, and re-layouts  30.1 us (5%)
  between operations  13.8 us (2%)
  other arithmetic  7.03 us (1%)
    ppermute x16, waiting for transfers between devices, swap(): lax.ppermute(array, 'ladder', [(source, source ^ flip) for source in rang...  258 us
    pallas_call x6, Pallas kernels, products(): pl.pallas_call(functools.partial(products_kernel, float(pairs * virt) **...  176 us
    ppermute x16, starting transfers between devices, swap(): lax.ppermute(array, 'ladder', [(source, source ^ flip) for source in rang...  103 us
    dynamic_slice x7, local copies, waits for them, and re-layouts, cut(): lax.dynamic_slice_in_dim(factors, (index ^ flip) * per_hub + begin, size, 0)  22.8 us
    all_gather x1, waiting for transfers between devices, per_device(): lam_all = lax.all_gather(lambdas, 'pair', axis=1, tiled=True)  14.2 us
  transfers between devices with their start and end apart: 21, of which 10 were waited for; matrix products, arithmetic and copies ran while one was open for 5% of the time, Pallas kernels for 27%

profile of v1, /device:TPU:0, one launch (start us, length us, event | category | flops | bytes accessed | tf_op | source)
XLA Modules:
  0.0 619.6 jit_solution(12442976711696021849)
XLA Ops:
  9.8 4.1 collective-permute-start
  15.2 4.3 constant_dynamic-slice_fusion.12
  19.5 6.2 constant_dynamic-slice_fusion.14
  25.7 14.2 %all-gather.2.cloned.1.call-done = bf16[4,512,512]{2,0,1:T(4,128)(2,1)} async-done(((bf16[4,64,512]{2,0,1:T(4,128)(2,1)}), bf16[4,512,512]{2,0,1:T(4,128)(2,1)}) %all-gather.2.cloned.1.call-update) | async-done | bytes 2097168 | tf_op jit(solution)/shard_map/all_gather | solution.py:164
  39.9 9.2 %collective-permute-done.refs_2_ = bf16[4,128,512]{2,1,0:T(8,128)(2,1)S(1)} collective-permute-done((bf16[4,128,512]{2,1,0:T(8,128)(2,1)S(1)}, bf16[4,128,512]{2,1,0:T(8,128)(2,1)S(1)}, u32[]{:S(2)}, u32[]{:S(2)}) %collective-permute-start) | collective-permute-done | bytes 524320 | tf_op jit(solution)/shard_map/ppermute | solution.py:152
  49.1 11.1 %collective-permute-start.2 = (bf16[48,128,512]{2,1,0:T(8,128)(2,1)}, bf16[48,128,512]{2,1,0:T(8,128)(2,1)}, u32[]{:S(2)}, u32[]{:S(2)}) collective-permute-start(bf16[48,128,512]{2,1,0:T(8,128)(2,1)} %constant_dynamic-slice_fusion.14), channel_id=1, source_target_pairs={{0,1},{1,0},{2,3},{3,2},{4,5},{5,4},{6,7},{7,6},{8,9},{9,8},{10,11... | collective-permute-start | bytes 18874376 | tf_op jit(solution)/shard_map/ppermute | solution.py:152
  60.2 1.9 collective-permute-start.3
  63.6 3.9 constant_dynamic-slice_fusion.6
  67.6 2.0 collective-permute-start.5
  70.6 3.0 copy.12
  73.5 5.4 convert_reduce_fusion
  79.1 229.5 %collective-permute-done.2.refs_1_ = bf16[48,128,512]{2,1,0:T(8,128)(2,1)} collective-permute-done((bf16[48,128,512]{2,1,0:T(8,128)(2,1)}, bf16[48,128,512]{2,1,0:T(8,128)(2,1)}, u32[]{:S(2)}, u32[]{:S(2)}) %collective-permute-start.2) | collective-permute-done | bytes 6291488 | tf_op jit(solution)/shard_map/ppermute | solution.py:152
  308.6 16.7 %shard_map.28.refs_6_ = f32[4,512,512]{2,1,0:T(8,128)} custom-call(s32[6]{0:T(128)S(1)} %stack.27.offset_ref, bf16[192,128,512]{2,1,0:T(8,128)(2,1)} %refs_0_.11, bf16[48,128,512]{2,1,0:T(8,128)(2,1)} %collective-permute-done.2.refs_1_, bf16[4,128,512]{2,1,0:T(8,128)(2,1)S(1)} %copy-done.3, bf16[4,128,512]{2,1,0:T(8,128)(2,1)S(1)} %copy-done.5, ...), custom_call_target="tpu_custom_call" | custom-call | flops 1 | bytes 1 | tf_op jit(solution)/shard_map/pallas_call | solution.py:123
  325.4 3.4 constant_dynamic-slice_fusion.4
  328.8 1.9 collective-permute-start.7
  330.8 2.1 collective-permute-start.8
  332.8 46.9 %shard_map.29.refs_6_ = f32[4,512,512]{2,1,0:T(8,128)} custom-call(s32[6]{0:T(128)S(1)} %stack.27.offset_ref, bf16[192,128,512]{2,1,0:T(8,128)(2,1)} %refs_0_.11, bf16[48,128,512]{2,1,0:T(8,128)(2,1)} %collective-permute-done.2.refs_1_, bf16[14,128,512]{2,1,0:T(8,128)(2,1)} %collective-permute-done.3.refs_2_, ...), custom_call_target="tpu_custom_call", output_to_operand_aliasing={{}: (7, {})} | custom-call | flops 1 | bytes 1 | tf_op jit(solution)/shard_map/pallas_call | solution.py:123
  379.7 2.6 constant_dynamic-slice_fusion
  382.4 36.1 %collective-permute-start.11 = (bf16[6,128,512]{2,1,0:T(8,128)(2,1)}, bf16[6,128,512]{2,1,0:T(8,128)(2,1)}, u32[]{:S(2)}, u32[]{:S(2)}) collective-permute-start(bf16[6,128,512]{2,1,0:T(8,128)(2,1)} %get-tuple-element.68), channel_id=1, source_target_pairs={{0,2},{1,3},{2,0},{3,1},{4,6},{5,7},{6,4},{7,5},{8,10},{9,11},{10,... | collective-permute-start | bytes 2359304 | tf_op jit(solution)/shard_map/ppermute | solution.py:152
  418.9 41.4 %shard_map.30.refs_6_ = f32[4,512,512]{2,1,0:T(8,128)} custom-call(s32[6]{0:T(128)S(1)} %stack.27.offset_ref, bf16[192,128,512]{2,1,0:T(8,128)(2,1)} %refs_0_.11, bf16[48,128,512]{2,1,0:T(8,128)(2,1)} %collective-permute-done.2.refs_1_, bf16[12,128,512]{2,1,0:T(8,128)(2,1)} %collective-permute-done.5.refs_2_, ...), custom_call_target="tpu_custom_call", output_to_operand_aliasing={{}: (7, {})} | custom-call | flops 1 | bytes 1 | tf_op jit(solution)/shard_map/pallas_call | solution.py:123
  460.3 14.9 %collective-permute-done.7.refs_2_ = bf16[10,128,512]{2,1,0:T(8,128)(2,1)} collective-permute-done((bf16[10,128,512]{2,1,0:T(8,128)(2,1)}, bf16[10,128,512]{2,1,0:T(8,128)(2,1)}, u32[]{:S(2)}, u32[]{:S(2)}) %collective-permute-start.7) | collective-permute-done | bytes 1310752 | tf_op jit(solution)/shard_map/ppermute | solution.py:152
  476.2 30.6 %collective-permute-start.9 = (bf16[2,128,512]{2,1,0:T(8,128)(2,1)S(1)}, bf16[2,128,512]{2,1,0:T(8,128)(2,1)S(1)}, u32[]{:S(2)}, u32[]{:S(2)}) collective-permute-start(bf16[2,128,512]{2,1,0:T(8,128)(2,1)S(1)} %get-tuple-element.70), channel_id=1, source_target_pairs={{0,2},{1,3},{2,0},{3,1},{4,6},{5,7},{6,4},{7,5},{8,10},{9,11},{10,... | collective-permute-start | bytes 786440 | tf_op jit(solution)/shard_map/ppermute | solution.py:152
  507.3 35.7 %shard_map.31.refs_6_ = f32[4,512,512]{2,1,0:T(8,128)} custom-call(s32[6]{0:T(128)S(1)} %stack.27.offset_ref, bf16[192,128,512]{2,1,0:T(8,128)(2,1)} %refs_0_.11, bf16[48,128,512]{2,1,0:T(8,128)(2,1)} %collective-permute-done.2.refs_1_, bf16[10,128,512]{2,1,0:T(8,128)(2,1)} %collective-permute-done.7.refs_2_, ...), custom_call_target="tpu_custom_call", output_to_operand_aliasing={{}: (7, {})} | custom-call | flops 1 | bytes 1 | tf_op jit(solution)/shard_map/pallas_call | solution.py:123
  543.0 24.3 %shard_map.32.refs_6_ = f32[4,512,512]{2,1,0:T(8,128)} custom-call(s32[6]{0:T(128)S(1)} %stack.27.offset_ref, bf16[192,128,512]{2,1,0:T(8,128)(2,1)} %refs_0_.11, bf16[48,128,512]{2,1,0:T(8,128)(2,1)} %collective-permute-done.2.refs_1_, bf16[6,128,512]{2,1,0:T(8,128)(2,1)} %collective-permute-done.11.refs_2_, ...), custom_call_target="tpu_custom_call", output_to_operand_aliasing={{}: (7, {})} | custom-call | flops 1 | bytes 1 | tf_op jit(solution)/shard_map/pallas_call | solution.py:123
  567.3 11.0 %shard_map.33 = (f32[4,4,1,64,512]{4,3,2,1,0:T(8,128)S(1)}, bf16[4,4,1,64,512]{4,3,2,1,0:T(8,128)(2,1)}) custom-call(s32[6]{0:T(128)S(1)} %stack.27.offset_ref, bf16[192,128,512]{2,1,0:T(8,128)(2,1)} %refs_0_.11, bf16[48,128,512]{2,1,0:T(8,128)(2,1)} %collective-permute-done.2.refs_1_, bf16[2,128,512]{2,1,0:T(8,128)(2,1)S(1)} %collective-permute-done.9.refs_2_, ...), custom_call_target="tpu_custom_call" | custom-call | flops 1 | bytes 1 | tf_op jit(solution)/shard_map/pallas_call | solution.py:123
  578.4 2.9 collective-permute-done.13
  583.1 2.5 collective-permute-start.16
  586.6 6.6 %collective-permute-done.16 = bf16[4,64,512]{2,1,0:T(8,128)(2,1)S(1)} collective-permute-done((bf16[4,64,512]{2,1,0:T(8,128)(2,1)S(1)}, bf16[4,64,512]{2,1,0:T(8,128)(2,1)S(1)}, u32[]{:S(2)}, u32[]{:S(2)}) %collective-permute-start.16) | collective-permute-done | bytes 262176 | tf_op jit(solution)/shard_map/ppermute | solution.py:221
  593.2 4.8 collective-permute-done.15
  599.4 3.5 collective-permute-start.19
  602.8 4.4 collective-permute-start.18
  607.7 3.8 collective-permute-done.18
  (50 shorter events, 14.9 us)
Async XLA Ops:
  6.5 33.3 %all-gather.2.cloned.1.call-start = ((), (), s32[]{:S(2)}) async-start(), calls=%async_computation | async-start | bytes 2359296 | tf_op jit(solution)/shard_map/all_gather | solution.py:164
  9.8 39.3 %collective-permute-start = (bf16[4,128,512]{2,1,0:T(8,128)(2,1)S(1)}, bf16[4,128,512]{2,1,0:T(8,128)(2,1)S(1)}, u32[]{:S(2)}, u32[]{:S(2)}) collective-permute-start(bf16[4,128,512]{2,1,0:T(8,128)(2,1)S(1)} %get-tuple-element.78), channel_id=1, source_target_pairs={{0,2},{1,3},{2,0},{3,1},{4,6},{5,7},{6,4},{7,5},{8,10},{9,11},{10,... | collective-permute-start | bytes 1572872 | tf_op jit(solution)/shard_map/ppermute | solution.py:152
  13.9 35.2 %collective-permute-start.1 = (bf16[4,128,512]{2,1,0:T(8,128)(2,1)S(1)}, bf16[4,128,512]{2,1,0:T(8,128)(2,1)S(1)}, u32[]{:S(2)}, u32[]{:S(2)}) collective-permute-start(bf16[4,128,512]{2,1,0:T(8,128)(2,1)S(1)} %get-tuple-element.77), channel_id=1, source_target_pairs={{0,3},{1,2},{2,1},{3,0},{4,7},{5,6},{6,5},{7,4},{8,11},{9,10},{10,... | collective-permute-start | bytes 1572872 | tf_op jit(solution)/shard_map/ppermute | solution.py:152
  49.1 18.5 %copy-start.2 = (bf16[4,128,512]{2,1,0:T(8,128)(2,1)}, bf16[4,128,512]{2,1,0:T(8,128)(2,1)S(1)}, u32[]{:S(2)}) copy-start(bf16[4,128,512]{2,1,0:T(8,128)(2,1)S(1)} %collective-permute-done.refs_2_) | copy-start | bytes 1572868
  49.1 18.5 %copy-start.4 = (bf16[4,128,512]{2,1,0:T(8,128)(2,1)}, bf16[4,128,512]{2,1,0:T(8,128)(2,1)S(1)}, u32[]{:S(2)}) copy-start(bf16[4,128,512]{2,1,0:T(8,128)(2,1)S(1)} %collective-permute-done.1.refs_3_) | copy-start | bytes 1572868
  49.1 259.5 %collective-permute-start.2 = (bf16[48,128,512]{2,1,0:T(8,128)(2,1)}, bf16[48,128,512]{2,1,0:T(8,128)(2,1)}, u32[]{:S(2)}, u32[]{:S(2)}) collective-permute-start(bf16[48,128,512]{2,1,0:T(8,128)(2,1)} %constant_dynamic-slice_fusion.14), channel_id=1, source_target_pairs={{0,1},{1,0},{2,3},{3,2},{4,5},{5,4},{6,7},{7,6},{8,9},{9,8},{10,11... | collective-permute-start | bytes 18874376 | tf_op jit(solution)/shard_map/ppermute | solution.py:152
  60.2 265.1 %collective-permute-start.3 = (bf16[14,128,512]{2,1,0:T(8,128)(2,1)}, bf16[14,128,512]{2,1,0:T(8,128)(2,1)}, u32[]{:S(2)}, u32[]{:S(2)}) collective-permute-start(bf16[14,128,512]{2,1,0:T(8,128)(2,1)} %get-tuple-element.47), channel_id=1, source_target_pairs={{0,2},{1,3},{2,0},{3,1},{4,6},{5,7},{6,4},{7,5},{8,10},{9,11},{10,... | collective-permute-start | bytes 5505032 | tf_op jit(solution)/shard_map/ppermute | solution.py:152
  62.1 263.2 %collective-permute-start.4 = (bf16[14,128,512]{2,1,0:T(8,128)(2,1)}, bf16[14,128,512]{2,1,0:T(8,128)(2,1)}, u32[]{:S(2)}, u32[]{:S(2)}) collective-permute-start(bf16[14,128,512]{2,1,0:T(8,128)(2,1)} %get-tuple-element.48), channel_id=1, source_target_pairs={{0,3},{1,2},{2,1},{3,0},{4,7},{5,6},{6,5},{7,4},{8,11},{9,10},{10,... | collective-permute-start | bytes 5505032 | tf_op jit(solution)/shard_map/ppermute | solution.py:152
  67.6 312.2 %collective-permute-start.5 = (bf16[12,128,512]{2,1,0:T(8,128)(2,1)}, bf16[12,128,512]{2,1,0:T(8,128)(2,1)}, u32[]{:S(2)}, u32[]{:S(2)}) collective-permute-start(bf16[12,128,512]{2,1,0:T(8,128)(2,1)} %get-tuple-element.74), channel_id=1, source_target_pairs={{0,2},{1,3},{2,0},{3,1},{4,6},{5,7},{6,4},{7,5},{8,10},{9,11},{10,... | collective-permute-start | bytes 4718600 | tf_op jit(solution)/shard_map/ppermute | solution.py:152
  69.6 310.1 %collective-permute-start.6 = (bf16[12,128,512]{2,1,0:T(8,128)(2,1)}, bf16[12,128,512]{2,1,0:T(8,128)(2,1)}, u32[]{:S(2)}, u32[]{:S(2)}) collective-permute-start(bf16[12,128,512]{2,1,0:T(8,128)(2,1)} %get-tuple-element.73), channel_id=1, source_target_pairs={{0,3},{1,2},{2,1},{3,0},{4,7},{5,6},{6,5},{7,4},{8,11},{9,10},{10,... | collective-permute-start | bytes 4718600 | tf_op jit(solution)/shard_map/ppermute | solution.py:152
  73.5 235.1 %copy-start = (bf16[4,512,512]{1,2,0:T(8,128)(2,1)}, bf16[4,512,512]{1,2,0:T(8,128)(2,1)S(1)}, u32[]{:S(2)}) copy-start(bf16[4,512,512]{1,2,0:T(8,128)(2,1)S(1)} %copy.12) | copy-start | bytes 6291460
  78.9 229.7 %copy-start.3 = (bf16[4,128,512]{2,1,0:T(8,128)(2,1)S(1)}, bf16[4,128,512]{2,1,0:T(8,128)(2,1)}, u32[]{:S(2)}) copy-start(bf16[4,128,512]{2,1,0:T(8,128)(2,1)} %copy-done.2) | copy-start | bytes 1572868
  78.9 229.7 %copy-start.5 = (bf16[4,128,512]{2,1,0:T(8,128)(2,1)S(1)}, bf16[4,128,512]{2,1,0:T(8,128)(2,1)}, u32[]{:S(2)}) copy-start(bf16[4,128,512]{2,1,0:T(8,128)(2,1)} %copy-done.4) | copy-start | bytes 1572868
  328.8 146.4 %collective-permute-start.7 = (bf16[10,128,512]{2,1,0:T(8,128)(2,1)}, bf16[10,128,512]{2,1,0:T(8,128)(2,1)}, u32[]{:S(2)}, u32[]{:S(2)}) collective-permute-start(bf16[10,128,512]{2,1,0:T(8,128)(2,1)} %get-tuple-element.72), channel_id=1, source_target_pairs={{0,2},{1,3},{2,0},{3,1},{4,6},{5,7},{6,4},{7,5},{8,10},{9,11},{10,... | collective-permute-start | bytes 3932168 | tf_op jit(solution)/shard_map/ppermute | solution.py:152
  330.8 144.4 %collective-permute-start.8 = (bf16[10,128,512]{2,1,0:T(8,128)(2,1)}, bf16[10,128,512]{2,1,0:T(8,128)(2,1)}, u32[]{:S(2)}, u32[]{:S(2)}) collective-permute-start(bf16[10,128,512]{2,1,0:T(8,128)(2,1)} %get-tuple-element.71), channel_id=1, source_target_pairs={{0,3},{1,2},{2,1},{3,0},{4,7},{5,6},{6,5},{7,4},{8,11},{9,10},{10,... | collective-permute-start | bytes 3932168 | tf_op jit(solution)/shard_map/ppermute | solution.py:152
  382.4 160.6 %collective-permute-start.11 = (bf16[6,128,512]{2,1,0:T(8,128)(2,1)}, bf16[6,128,512]{2,1,0:T(8,128)(2,1)}, u32[]{:S(2)}, u32[]{:S(2)}) collective-permute-start(bf16[6,128,512]{2,1,0:T(8,128)(2,1)} %get-tuple-element.68), channel_id=1, source_target_pairs={{0,2},{1,3},{2,0},{3,1},{4,6},{5,7},{6,4},{7,5},{8,10},{9,11},{10,... | collective-permute-start | bytes 2359304 | tf_op jit(solution)/shard_map/ppermute | solution.py:152
  418.5 124.5 %collective-permute-start.12 = (bf16[6,128,512]{2,1,0:T(8,128)(2,1)}, bf16[6,128,512]{2,1,0:T(8,128)(2,1)}, u32[]{:S(2)}, u32[]{:S(2)}) collective-permute-start(bf16[6,128,512]{2,1,0:T(8,128)(2,1)} %get-tuple-element.67), channel_id=1, source_target_pairs={{0,3},{1,2},{2,1},{3,0},{4,7},{5,6},{6,5},{7,4},{8,11},{9,10},{10,... | collective-permute-start | bytes 2359304 | tf_op jit(solution)/shard_map/ppermute | solution.py:152
  418.9 88.4 %copy-start.1 = (bf16[4,512,512]{1,2,0:T(8,128)(2,1)S(1)}, bf16[4,512,512]{1,2,0:T(8,128)(2,1)}, u32[]{:S(2)}) copy-start(bf16[4,512,512]{1,2,0:T(8,128)(2,1)} %copy-done) | copy-start | bytes 6291460
  476.2 91.1 %collective-permute-start.9 = (bf16[2,128,512]{2,1,0:T(8,128)(2,1)S(1)}, bf16[2,128,512]{2,1,0:T(8,128)(2,1)S(1)}, u32[]{:S(2)}, u32[]{:S(2)}) collective-permute-start(bf16[2,128,512]{2,1,0:T(8,128)(2,1)S(1)} %get-tuple-element.70), channel_id=1, source_target_pairs={{0,2},{1,3},{2,0},{3,1},{4,6},{5,7},{6,4},{7,5},{8,10},{9,11},{10,... | collective-permute-start | bytes 786440 | tf_op jit(solution)/shard_map/ppermute | solution.py:152
  506.9 60.4 %collective-permute-start.10 = (bf16[2,128,512]{2,1,0:T(8,128)(2,1)S(1)}, bf16[2,128,512]{2,1,0:T(8,128)(2,1)S(1)}, u32[]{:S(2)}, u32[]{:S(2)}) collective-permute-start(bf16[2,128,512]{2,1,0:T(8,128)(2,1)S(1)} %get-tuple-element.69), channel_id=1, source_target_pairs={{0,3},{1,2},{2,1},{3,0},{4,7},{5,6},{6,5},{7,4},{8,11},{9,10},{10,... | collective-permute-start | bytes 786440 | tf_op jit(solution)/shard_map/ppermute | solution.py:152
  578.3 2.9 collective-permute-start.13
  581.6 1.4 copy-start.6
  583.1 10.2 %collective-permute-start.16 = (bf16[4,64,512]{2,1,0:T(8,128)(2,1)S(1)}, bf16[4,64,512]{2,1,0:T(8,128)(2,1)S(1)}, u32[]{:S(2)}, u32[]{:S(2)}) collective-permute-start(bf16[4,64,512]{2,1,0:T(8,128)(2,1)S(1)} %get-tuple-element.80), channel_id=1, source_target_pairs={{0,24},{4,28},{8,16},{12,20},{16,8},{20,12},{24,0},{28,4},{1,25},{... | collective-permute-start | bytes 786440 | tf_op jit(solution)/shard_map/ppermute | solution.py:221
  585.6 12.4 %collective-permute-start.15 = (bf16[4,64,512]{2,1,0:T(8,128)(2,1)S(1)}, bf16[4,64,512]{2,1,0:T(8,128)(2,1)S(1)}, u32[]{:S(2)}, u32[]{:S(2)}) collective-permute-start(bf16[4,64,512]{2,1,0:T(8,128)(2,1)S(1)} %get-tuple-element.81), channel_id=1, source_target_pairs={{0,16},{4,20},{8,24},{12,28},{16,0},{20,4},{24,8},{28,12},{1,17},{... | collective-permute-start | bytes 786440 | tf_op jit(solution)/shard_map/ppermute | solution.py:221
  586.1 12.0 %collective-permute-start.14 = (bf16[4,64,512]{2,1,0:T(8,128)(2,1)S(1)}, bf16[4,64,512]{2,1,0:T(8,128)(2,1)S(1)}, u32[]{:S(2)}, u32[]{:S(2)}) collective-permute-start(bf16[4,64,512]{2,1,0:T(8,128)(2,1)S(1)} %get-tuple-element.79), channel_id=1, source_target_pairs={{0,8},{4,12},{8,0},{12,4},{16,24},{20,28},{24,16},{28,20},{1,9},{5... | collective-permute-start | bytes 786440 | tf_op jit(solution)/shard_map/ppermute | solution.py:221
  599.4 8.3 %collective-permute-start.19 = (bf16[4,64,128]{2,1,0:T(8,128)(2,1)S(1)}, bf16[4,64,128]{2,1,0:T(8,128)(2,1)S(1)}, u32[]{:S(2)}, u32[]{:S(2)}) collective-permute-start(bf16[4,64,128]{2,1,0:T(8,128)(2,1)S(1)} %get-tuple-element.87), channel_id=1, source_target_pairs={{0,3},{1,2},{2,1},{3,0},{4,7},{5,6},{6,5},{7,4},{8,11},{9,10},{10,... | collective-permute-start | bytes 196616 | tf_op jit(solution)/shard_map/ppermute | solution.py:152
  602.8 8.7 %collective-permute-start.18 = (bf16[4,64,128]{2,1,0:T(8,128)(2,1)S(1)}, bf16[4,64,128]{2,1,0:T(8,128)(2,1)S(1)}, u32[]{:S(2)}, u32[]{:S(2)}) collective-permute-start(bf16[4,64,128]{2,1,0:T(8,128)(2,1)S(1)} %get-tuple-element.88), channel_id=1, source_target_pairs={{0,2},{1,3},{2,0},{3,1},{4,6},{5,7},{6,4},{7,5},{8,10},{9,11},{10,... | collective-permute-start | bytes 196616 | tf_op jit(solution)/shard_map/ppermute | solution.py:152
  607.2 4.6 collective-permute-start.17
Sparse Core Ops, SparseCore 0:
  9.2 30.5 all-gather.1
